TPU v7x, 768 devices: a whole 4x8x12 slice. The times are simulated.
768 devices in a mesh: path: 12 (over x, z_hi), fsdp: 64 (over y, z_lo, core).
Axes of the slice: x: 4, y: 8, z: 12 (z_hi: 3, z_lo: 4; z = z_hi * 4 + z_lo), core: 2. Of those that a mesh axis runs over, the one named last changes fastest.
Arguments:
- tokens: bfloat16 [12, 1024, 4096], P('path', 'fsdp'), may hold values from -6 to 6
- up_values: bfloat16 [12, 1024, 7680], P('path', None, 'fsdp'), may hold values from -6 to 6
- out_grad: bfloat16 [12, 1024, 7680], P('path', None, 'fsdp'), may hold values from -6 to 6
- weights: bfloat16 [12, 4096, 7680], P('path', None, 'fsdp'), may hold values from -6 to 6
- momentum: float32 [12, 4096, 7680], P('path', None, 'fsdp'), may hold values from -1.5 to 1.5
- path_table: int32 [12, 1], replicated, may hold values from 0 to 15, as said below
- live_tokens: int32 [12], P('path'), may hold values from 256 to 1024, as said below
Outputs:
- new_weights: bfloat16 [12, 4096, 7680], P('path', None, 'fsdp')
Inputs may be any that keep to these rules, and one draw needn't show every extreme that they name: `path_table`: module ids of the level; several groups share some modules, others hold a module alone. Routed tokens fill positions 0 to live_tokens[g] - 1 of a group's block.
All inputs are finite; a program needn't handle non-finite values.
Results may differ from a plain program's by a relative error of at most 0.0034.
Values may be sent and summed in bfloat16 or wider, within the bound.
A program may use at most 64 MiB of HBM per device.

v0:
```python
import jax
import jax.numpy as jnp
from jax import lax
from jax.sharding import PartitionSpec as P

D = 4096


def average_groups(block, share, count):
    summed = jnp.einsum(
        "gh,hdc->gdc",
        share,
        lax.all_to_all(block, "path", split_axis=2, concat_axis=0, tiled=True),
        preferred_element_type=jnp.float32,
    )
    mixed = (summed / count[:, None, None]).astype(jnp.bfloat16)
    return lax.all_to_all(mixed, "path", split_axis=0, concat_axis=2, tiled=True)


def on_device(tokens, up_values, out_grad, weights, momentum, path_table, live_tokens):
    scale = 1.0 / D**0.5
    local_rows = tokens[0]
    weight_now = weights[0]
    up_rows = up_values[0]
    grad_rows = out_grad[0]
    live = live_tokens[0]
    gathered = lax.all_gather(local_rows, "fsdp", axis=0, tiled=True)
    length = gathered.shape[0]
    gate = jnp.dot(gathered, weight_now, preferred_element_type=jnp.float32) * scale
    sig = jax.nn.sigmoid(gate)
    slope = sig * (1.0 + gate * (1.0 - sig))
    up_part = up_rows.astype(jnp.float32)
    grad_part = grad_rows.astype(jnp.float32)
    keep = jnp.arange(length, dtype=jnp.int32) < live
    gate_grad = jnp.where(keep[:, None], grad_part * up_part * slope, 0.0).astype(jnp.bfloat16)
    total = lax.dot_general(
        gathered, gate_grad, (((0,), (0,)), ((), ())), preferred_element_type=jnp.float32
    )
    pseudo = (total * scale).astype(jnp.bfloat16)[None]
    ids = path_table[:, 0]
    share = (ids[:, None] == ids[None, :]).astype(jnp.bfloat16)
    count = jnp.sum(share.astype(jnp.float32), axis=1)
    averaged = average_groups(pseudo, share, count)
    averaged = averaged.astype(jnp.float32)
    new_moment = 0.9 * momentum + averaged
    fresh = weights.astype(jnp.float32) - 0.7 * (averaged + 0.9 * new_moment)
    return fresh.astype(jnp.bfloat16)


def solution(mesh):
    return jax.shard_map(
        on_device,
        mesh=mesh,
        in_specs=(
            P("path", "fsdp", None),
            P("path", None, "fsdp"),
            P("path", None, "fsdp"),
            P("path", None, "fsdp"),
            P("path", None, "fsdp"),
            P(),
            P("path"),
        ),
        out_specs=P("path", None, "fsdp"),
        check_vma=False,
    )
```

profile of v0, /device:TPU:1, one launch (start us, length us, event | category | flops | bytes accessed | tf_op | source)
XLA Modules:
  0.0 288.9 jit_solution(14063920543316349246)
XLA Ops:
  6.5 0.0 all-gather.3.cloned.1.call-start
  6.5 0.7 all-gather.3.cloned.1.call-update
  7.9 138.2 %all-gather.3.cloned.1.call-done = bf16[1,1024,4096]{2,1,0:T(8,128)(2,1)} async-done(((bf16[1,16,4096]{2,1,0:T(8,128)(2,1)}), bf16[1,1024,4096]{2,1,0:T(8,128)(2,1)}) %all-gather.3.cloned.1.call-update) | async-done | bytes 8388624 | tf_op jit(solution)/shard_map/all_gather | solution.py:27
  146.1 10.4 %fusion.11 = bf16[1,4096,120]{1,2,0:T(8,128)(2,1)S(1)} fusion(bf16[1,1024,4096]{2,1,0:T(8,128)(2,1)} %all-gather.3.cloned.1.call-done, bf16[1,4096,120]{1,2,0:T(8,128)(2,1)} %param.10, bf16[1,1024,120]{1,2,0:T(8,128)(2,1)} %param.8, bf16[1,1024,120]{1,2,0:T(8,128)(2,1)} %param.9, pred[1024]{0:T(1024)(128)(4,1)S(1)} %iota_compare_fusion), kind=kOutput, calls=%fused_computation.8 | convolution fusion | flops 2015969280 | bytes 10847232 | tf_op jit(solution)/shard_map/dot_general | solution.py:36
  156.5 2.2 copy.33
  158.7 0.5 broadcast.21
  159.2 6.6 %reduce.2 = bf16[120,4096]{1,0:T(8,128)(2,1)S(1)} reduce(bf16[120,1,4096]{2,1,0:T(2,128)(2,1)S(1)} %bitcast.61, bf16[]{:T(256)} %broadcast.21), dimensions={1}, to_apply=%bitcast.59.reduce_sub_computation | reduce | bytes 1966082
  165.9 0.0 copy-start
  165.9 2.0 reshape.31
  167.9 9.3 %all-to-all-start = ((bf16[12,2,20480]{2,1,0:T(2,128)(2,1)}), bf16[12,2,20480]{2,1,0:T(2,128)(2,1)S(1)}, u32[]{:S(2)}, u32[]{:S(2)}) async-start(bf16[12,2,20480]{2,1,0:T(2,128)(2,1)} %reshape.31), calls=%async_computation | async-start | bytes 1966080 | tf_op jit(solution)/shard_map/all_to_all | solution.py:13
  177.2 0.0 copy-done
  177.2 0.2 convert_reduce_fusion
  177.4 36.8 %all-to-all-done = bf16[12,2,20480]{2,1,0:T(2,128)(2,1)S(1)} async-done(((bf16[12,2,20480]{2,1,0:T(2,128)(2,1)}), bf16[12,2,20480]{2,1,0:T(2,128)(2,1)S(1)}, u32[]{:S(2)}, u32[]{:S(2)}) %all-to-all-start) | async-done | bytes 983072 | tf_op jit(solution)/shard_map/all_to_all | solution.py:13
  214.2 1.0 reshape.32
  215.2 5.8 %bitcast_reduce_fusion = bf16[4096,120]{0,1:T(8,128)(2,1)S(1)} fusion(bf16[120,1,4096]{2,1,0:T(2,128)(2,1)S(1)} %reshape.32), kind=kLoop, calls=%fused_computation.34 | loop fusion | bytes 1966080 | tf_op jit(solution)/shard_map/all_to_all | solution.py:13
  221.0 0.3 all_to_all.21
  221.3 1.2 fusion.4
  222.5 0.6 copy.24
  223.2 53.2 %all_to_all.27 = bf16[12,4096,10]{1,2,0:T(8,128)(2,1)S(1)} all-to-all(bf16[12,4096,10]{1,2,0:T(8,128)(2,1)S(1)} %copy.24), channel_id=1, replica_groups=mesh['path'=12,'fsdp'=64] {'path'}, dimensions={0} | all-to-all | bytes 1966080 | tf_op jit(solution)/shard_map/all_to_all | solution.py:17
  276.3 0.3 convert_bitcast_fusion
  276.7 1.6 reshape.29
  278.2 3.8 %subtract_convert_fusion = bf16[1,4096,120]{1,2,0:T(8,128)(2,1)} fusion(f32[1,4096,120]{1,2,0:T(8,128)} %reshape.29, f32[1,4096,120]{1,2,0:T(8,128)} %param.11, bf16[1,4096,120]{1,2,0:T(8,128)(2,1)} %param.10), kind=kLoop, calls=%fused_computation.10 | loop fusion | flops 3932160 | bytes 5898240 | tf_op jit(solution)/shard_map/convert_element_type | solution.py:47
  (1 shorter events, 0.0 us)
Async XLA Ops:
  6.5 139.6 %all-gather.3.cloned.1.call-start = ((), (), s32[]{:S(2)}) async-start(), calls=%async_computation.2 | async-start | bytes 8519680 | tf_op jit(solution)/shard_map/all_gather | solution.py:27
  165.9 11.3 %copy-start = (s32[12,1]{0,1:T(1,128)S(1)}, s32[12,1]{0,1:T(1,128)}, u32[]{:S(2)}) copy-start(s32[12,1]{0,1:T(1,128)} %param.12) | copy-start | bytes 148
  167.9 46.3 %all-to-all-start = ((bf16[12,2,20480]{2,1,0:T(2,128)(2,1)}), bf16[12,2,20480]{2,1,0:T(2,128)(2,1)S(1)}, u32[]{:S(2)}, u32[]{:S(2)}) async-start(bf16[12,2,20480]{2,1,0:T(2,128)(2,1)} %reshape.31), calls=%async_computation | async-start | bytes 1966080 | tf_op jit(solution)/shard_map/all_to_all | solution.py:13
Sparse Core Ops, SparseCore 0:
  9.8 136.2 all-gather.2
where the time goes:
time: 289 us
  waiting for transfers between devices  176 us (61%)
  blocking collectives  53.2 us (18%)
  local copies, waits for them, and re-layouts  14.1 us (5%)
  between operations  14.1 us (5%)
  matrix products  11.6 us (4%)
  other arithmetic  11 us (4%)
  starting transfers between devices  9.26 us (3%)
    all_gather x1, waiting for transfers between devices, on_device(): gathered = lax.all_gather(local_rows, 'fsdp', axis=0, tiled=True)  138 us
    all_to_all x1, blocking collectives, average_groups(): lax.all_to_all(mixed, 'path', split_axis=0, concat_axis=2, tiled=True)  53.2 us
    all_to_all x1, waiting for transfers between devices, average_groups(): lax.all_to_all(block, 'path', split_axis=2, concat_axis=0, tiled=True)  36.8 us
    dot_general x1, matrix products, on_device(): lax.dot_general(gathered, gate_grad, (((0,), (0,)), ((), ())), preferred_...  10.4 us
    all_to_all x1, starting transfers between devices, average_groups(): lax.all_to_all(block, 'path', split_axis=2, concat_axis=0, tiled=True)  9.26 us
    unnamed x1, other arithmetic  6.62 us
    all_to_all x2, local copies, waits for them, and re-layouts, average_groups(): lax.all_to_all(block, 'path', split_axis=2, concat_axis=0, tiled=True)  6.15 us
  transfers between devices with their start and end apart: 2, of which 2 were waited for; matrix products, arithmetic and copies ran while one was open for 0% of the time, Pallas kernels for 0%

commit v1 on v0

v1 whole, which is shorter than its diff:
```python
import jax
import jax.numpy as jnp
from jax import lax
from jax.experimental import pallas as pl
from jax.experimental.pallas import tpu as pltpu
from jax.sharding import PartitionSpec as P

MESH = pl.DeviceIdType.MESH

NX, ZH, NY, ZL = 4, 3, 8, 4
NP = NX * ZH
D, TOK, COLS = 4096, 1024, 120
ROWS = TOK // (NY * ZL * 2)
BUNDLE = ROWS * ZL * 2
QUARTER = D // NX
THIRD = COLS // ZH
CHUNKS = 2
LANES = 256
PART = THIRD * QUARTER // (CHUNKS * LANES)
SUBS = PART // THIRD

SLOT = {0: 0, 4: 1, 1: 2, -1: 3, 2: 4, -2: 5, 3: 6, -3: 7}


def body(
    tok_in, up_in, og_in, w_in, mom_in, table, live, out,
    tok, up, og, w, mom, acc, psend, precv, asend, arecv, fresh, share, inv,
    load_sem, own_sem, z_send, z_recv, y_send, y_recv, c_send, c_recv,
    p_send, p_recv, a_send, a_recv, out_sem,
):
    path = lax.axis_index("path")
    fsdp = lax.axis_index("fsdp")
    core = fsdp % 2
    z = (fsdp // 2) % ZL
    y = fsdp // (2 * ZL)
    x = path // ZH
    third = path % ZH

    def at(yy, zz, cc):
        return (path, (yy * ZL + zz) * 2 + cc)

    order = (z, z + 1 - 2 * (z % 2), 2 - z // 2, 3 - 3 * (z // 2))
    up_y, down_y = at((y + 1) % NY, z, core), at((y + NY - 1) % NY, z, core)
    sibling = at(y, z, 1 - core)

    loads = [
        pltpu.make_async_copy(src, dst, load_sem.at[i])
        for i, (src, dst) in enumerate(((w_in, w), (up_in, up), (og_in, og), (mom_in, mom)))
    ]

    def rows(rel, k):
        return pl.ds(pl.multiple_of(SLOT[rel] * BUNDLE + (order[k] * 2 + core) * ROWS, ROWS), ROWS)

    own = pltpu.make_async_copy(tok_in, tok.at[rows(0, 0)], own_sem)
    own.start()
    for load in loads:
        load.start()

    barrier = pltpu.get_barrier_semaphore()
    friends = [up_y, down_y, sibling]
    friends += [at(y, order[k], core) for k in range(1, ZL)]
    friends += [((path + o) % NP, fsdp) for o in range(1, NP)]
    for friend in friends:
        pl.semaphore_signal(barrier, inc=1, device_id=friend, device_id_type=MESH)
    pl.semaphore_wait(barrier, len(friends))

    def z_copy(k):
        return pltpu.make_async_remote_copy(
            src_ref=tok_in, dst_ref=tok.at[rows(0, 0)], send_sem=z_send.at[k], recv_sem=z_recv.at[z],
            device_id=at(y, order[k], core), device_id_type=MESH,
        )

    def z_arrival(k):
        return pltpu.make_async_remote_copy(
            src_ref=tok_in, dst_ref=tok.at[rows(0, k)], send_sem=z_send.at[k], recv_sem=z_recv.at[order[k]],
            device_id=at(y, order[k], core), device_id_type=MESH,
        )

    def y_copy(way, step, k):
        sign = (-1, 1)[way]
        before, after = sign * (step - 1), sign * step
        after = 4 if after == -4 else after
        src = tok_in if step == 1 and k == 0 else tok.at[rows(before, k)]
        return pltpu.make_async_remote_copy(
            src_ref=src, dst_ref=tok.at[rows(after, k)],
            send_sem=y_send.at[way, step - 1, k], recv_sem=y_recv.at[way, step - 1, k],
            device_id=(up_y, down_y)[way], device_id_type=MESH,
        )

    def c_copy(rel, k):
        src = tok_in if rel == 0 and k == 0 else tok.at[rows(rel, k)]
        return pltpu.make_async_remote_copy(
            src_ref=src, dst_ref=tok.at[rows(rel, k)],
            send_sem=c_send.at[SLOT[rel], k], recv_sem=c_recv.at[SLOT[rel], k],
            device_id=sibling, device_id_type=MESH,
        )

    def sent(way, step, k):
        return step < 4 or (k < 2) == (way == 0)

    def gate_and_grad(rels, first):
        start, count = SLOT[rels[0]] * BUNDLE, len(rels) * BUNDLE
        gate = lax.dot_general(
            w[...], tok[start : start + count], (((1,), (1,)), ((), ())), preferred_element_type=jnp.float32
        ) * (1.0 / D**0.5)
        parts = []
        for i, rel in enumerate(rels):
            here = (y + rel + NY) % NY * BUNDLE
            lanes = pl.ds(pl.multiple_of(here, BUNDLE), BUNDLE)
            g = gate[:, i * BUNDLE : (i + 1) * BUNDLE]
            sig = jax.nn.sigmoid(g)
            slope = sig * (1.0 + g * (1.0 - sig))
            term = og[:, lanes].astype(jnp.float32) * up[:, lanes].astype(jnp.float32) * slope
            token = here + lax.broadcasted_iota(jnp.int32, (COLS, BUNDLE), 1)
            parts.append(jnp.where(token < live[0], term, 0.0).astype(jnp.bfloat16))
        return start, count, parts[0] if len(parts) == 1 else jnp.concatenate(parts, axis=1)

    def accumulate(rels, first):
        start, count, grad = gate_and_grad(rels, first)
        for q in range(NX):
            lanes = slice(q * QUARTER, (q + 1) * QUARTER)
            term = jnp.dot(grad, tok[start : start + count, lanes], preferred_element_type=jnp.float32)
            if first:
                acc[:, lanes] = term
            else:
                acc[:, lanes] += term

    def wait_sibling(rel):
        for k in range(ZL):
            c_copy(rel, k).wait_recv()

    for k in range(1, ZL):
        z_copy(k).start()
    for way in (0, 1):
        y_copy(way, 1, 0).start()
    c_copy(0, 0).start()
    for g in range(NP):
        total = jnp.float32(0.0)
        for h in range(NP):
            same = jnp.where(table[g] == table[h], 1.0, 0.0).astype(jnp.float32)
            share[g * NP + h] = same
            total = total + same
        inv[g] = 1.0 / total
    own.wait()
    for k in range(1, ZL):
        z_arrival(k).wait_recv()
        for way in (0, 1):
            y_copy(way, 1, k).start()
        c_copy(0, k).start()
    for load in loads[:3]:
        load.wait()

    def ring(step):
        for k in range(ZL):
            for way in (0, 1):
                if sent(way, step, k):
                    y_copy(way, step, k).wait_recv()
                    if step < 4 and sent(way, step + 1, k):
                        y_copy(way, step + 1, k).start()
                    c_copy((-1, 1)[way] * step if step < 4 else 4, k).start()

    wait_sibling(0)
    accumulate((0,), True)
    for step in (1, 2, 3):
        ring(step)
        if step > 1:
            wait_sibling(step - 1)
            wait_sibling(1 - step)
            accumulate((step - 1, 1 - step), False)
    wait_sibling(3)
    wait_sibling(-3)
    accumulate((3, -3), False)
    ring(4)
    wait_sibling(4)

    def p_copy(chunk, dest):
        return pltpu.make_async_remote_copy(
            src_ref=psend.at[chunk, dest], dst_ref=precv.at[chunk, path],
            send_sem=p_send.at[chunk, dest], recv_sem=p_recv.at[chunk, path],
            device_id=(dest, fsdp), device_id_type=MESH,
        )

    def p_arrival(chunk, source):
        return pltpu.make_async_remote_copy(
            src_ref=psend.at[chunk, source], dst_ref=precv.at[chunk, source],
            send_sem=p_send.at[chunk, source], recv_sem=p_recv.at[chunk, source],
            device_id=(source, fsdp), device_id_type=MESH,
        )

    def a_copy(chunk, dest):
        return pltpu.make_async_remote_copy(
            src_ref=asend.at[chunk, dest], dst_ref=arecv.at[chunk, path],
            send_sem=a_send.at[chunk, dest], recv_sem=a_recv.at[chunk, path],
            device_id=(dest, fsdp), device_id_type=MESH,
        )

    def a_arrival(chunk, source):
        return pltpu.make_async_remote_copy(
            src_ref=asend.at[chunk, source], dst_ref=arecv.at[chunk, source],
            send_sem=a_send.at[chunk, source], recv_sem=a_recv.at[chunk, source],
            device_id=(source, fsdp), device_id_type=MESH,
        )

    start, count, grad = gate_and_grad((4,), False)
    for j in range(NX):
        q = (x + j) % NX
        lanes = pl.ds(pl.multiple_of(q * QUARTER, QUARTER), QUARTER)
        total = acc[:, lanes] + jnp.dot(grad, tok[start : start + count, lanes], preferred_element_type=jnp.float32)
        total = total * (1.0 / D**0.5)
        for chunk in range(CHUNKS):
            for i in range(ZH):
                r = (third + 1 + i) % ZH
                dest = q * ZH + r
                first = chunk * SUBS * LANES
                for rr in range(ZH):
                    piece = jnp.concatenate(
                        [
                            total[rr * THIRD : (rr + 1) * THIRD, first + s * LANES : first + (s + 1) * LANES]
                            for s in range(SUBS)
                        ],
                        axis=0,
                    ).astype(jnp.bfloat16)
                    if i == 0:
                        psend[chunk, q * ZH + rr] = piece
                if j > 0 or i < ZH - 1:
                    p_copy(chunk, dest).start()

    for chunk in range(CHUNKS):
        for o in range(1, NP):
            p_arrival(chunk, (path + o) % NP).wait_recv()
        mine = pltpu.make_async_copy(psend.at[chunk, path], precv.at[chunk, path], own_sem)
        mine.start()
        mine.wait()

        @pl.loop(0, PART // 16)
        def _(i):
            part = pl.ds(pl.multiple_of(i * 16, 16), 16)
            values = [precv[chunk, h, part].astype(jnp.float32) for h in range(NP)]
            for g in range(NP):
                total = share[g * NP] * values[0]
                for h in range(1, NP):
                    total = total + share[g * NP + h] * values[h]
                asend[chunk, g, part] = (total * inv[g]).astype(jnp.bfloat16)

        for o in range(1, NP):
            a_copy(chunk, (path + o) % NP).start()

    loads[3].wait()
    writes = []
    for chunk in range(CHUNKS):
        mine = pltpu.make_async_copy(asend.at[chunk, path], arecv.at[chunk, path], own_sem)
        mine.start()
        mine.wait()
        for o in range(1, NP):
            a_arrival(chunk, (path + o) % NP).wait_recv()
        for q in range(NX):
            for s in range(SUBS):
                lanes = slice(q * QUARTER + (chunk * SUBS + s) * LANES, q * QUARTER + (chunk * SUBS + s + 1) * LANES)
                averaged = jnp.concatenate(
                    [
                        arecv[chunk, q * ZH + r].astype(jnp.float32)[s * THIRD : (s + 1) * THIRD]
                        for r in range(ZH)
                    ],
                    axis=0,
                )
                moment = 0.9 * mom[:, lanes] + averaged
                new = w[:, lanes].astype(jnp.float32) - 0.7 * (averaged + 0.9 * moment)
                fresh[:, lanes] = new.astype(jnp.bfloat16)
    write = pltpu.make_async_copy(fresh, out, out_sem)
    write.start()

    for k in range(1, ZL):
        z_copy(k).wait_send()
    for step in range(1, 5):
        for k in range(ZL):
            for way in (0, 1):
                if sent(way, step, k):
                    y_copy(way, step, k).wait_send()
    for rel in SLOT:
        for k in range(ZL):
            c_copy(rel, k).wait_send()
    for chunk in range(CHUNKS):
        for o in range(1, NP):
            p_copy(chunk, (path + o) % NP).wait_send()
            a_copy(chunk, (path + o) % NP).wait_send()
    write.wait()


def on_device(tokens, up_values, out_grad, weights, momentum, path_table, live_tokens):
    dma = pltpu.SemaphoreType.DMA
    bf16, f32 = jnp.bfloat16, jnp.float32
    anywhere = pl.BlockSpec(memory_space=pl.ANY)
    scalars = pl.BlockSpec(memory_space=pltpu.SMEM)
    shard = pltpu.VMEM((CHUNKS, NP, PART, LANES), bf16)
    new = pl.pallas_call(
        body,
        out_shape=jax.ShapeDtypeStruct((COLS, D), bf16),
        in_specs=[anywhere] * 5 + [scalars] * 2,
        out_specs=anywhere,
        scratch_shapes=[
            pltpu.VMEM((TOK, D), bf16),
            pltpu.VMEM((COLS, TOK), bf16),
            pltpu.VMEM((COLS, TOK), bf16),
            pltpu.VMEM((COLS, D), bf16),
            pltpu.VMEM((COLS, D), f32),
            pltpu.VMEM((COLS, D), f32),
            shard, shard, shard, shard,
            pltpu.VMEM((COLS, D), bf16),
            pltpu.SMEM((NP * NP,), f32),
            pltpu.SMEM((NP,), f32),
            dma((4,)),
            dma,
            dma((ZL,)), dma((ZL,)),
            dma((2, 4, ZL)), dma((2, 4, ZL)),
            dma((NY, ZL)), dma((NY, ZL)),
            dma((CHUNKS, NP)), dma((CHUNKS, NP)),
            dma((CHUNKS, NP)), dma((CHUNKS, NP)),
            dma,
        ],
        compiler_params=pltpu.CompilerParams(
            collective_id=0, has_side_effects=True, vmem_limit_bytes=40 * 2**20
        ),
        name="outer_step",
    )(
        tokens[0], up_values[0].T, out_grad[0].T, weights[0].T, momentum[0].T,
        path_table[:, 0], live_tokens,
    )
    return new.T[None]


def solution(mesh):
    return jax.shard_map(
        on_device,
        mesh=mesh,
        in_specs=(
            P("path", "fsdp", None),
            P("path", None, "fsdp"),
            P("path", None, "fsdp"),
            P("path", None, "fsdp"),
            P("path", None, "fsdp"),
            P(),
            P("path"),
        ),
        out_specs=P("path", None, "fsdp"),
        check_vma=False,
    )
```

time: 289 us -> 141 us (0.49)
  the two profiles are of different devices: /device:TPU:1 before, /device:TPU:56 now
where the time goes in v1:
time: 141 us; the launch traced here: 140 us
  Pallas kernels  132 us (94%)
  local copies, waits for them, and re-layouts  7.13 us (5%)
    pallas_call x1, Pallas kernels, on_device(): pl.pallas_call(body, out_shape=jax.ShapeDtypeStruct((COLS, D), bf16), in_...  132 us
    unnamed x13, local copies, waits for them, and re-layouts  7.13 us

profile of v1, /device:TPU:56, one launch (start us, length us, event | category | flops | bytes accessed | tf_op | source)
XLA Modules:
  0.0 139.7 jit_solution(5123555196513498763)
XLA Ops:
  0.7 0.0 copy-start
  0.7 1.5 %copy-done = f32[1,4096,120]{1,2,0:T(8,128)S(1)} copy-done((f32[1,4096,120]{1,2,0:T(8,128)S(1)}, f32[1,4096,120]{1,2,0:T(8,128)}, u32[]{:S(2)}) %copy-start) | copy-done | bytes 1966104
  2.2 0.0 copy-start.1
  2.2 1.2 copy-done.1
  3.4 0.0 copy-start.2
  3.4 0.9 copy-done.2
  4.3 0.0 copy-start.3
  4.3 0.9 copy-done.3
  5.3 0.0 copy-start.4
  5.3 0.9 copy-done.4
  6.2 0.0 copy-start.5
  6.2 0.7 copy-done.5
  6.9 131.9 %outer_step.1 = bf16[120,4096]{1,0:T(8,128)(2,1)S(1)} custom-call(bf16[16,4096]{1,0:T(8,128)(2,1)S(1)} %bitcast.22, bf16[120,1024]{1,0:T(8,128)(2,1)S(1)} %bitcast.20, bf16[120,1024]{1,0:T(8,128)(2,1)S(1)} %bitcast.21, bf16[120,4096]{1,0:T(8,128)(2,1)S(1)} %bitcast.19, f32[120,4096]{1,0:T(8,128)S(1)} %bitcast.18, s32[12]{0:T(128)S(1)} %bitcast.23, ...), custom_call_target="tpu_custom_call" | custom-call | tf_op jit(solution)/shard_map/outer_step/pallas_call | solution.py:295
  138.7 0.9 copy.10
Async XLA Ops:
  0.7 1.5 %copy-start = (f32[1,4096,120]{1,2,0:T(8,128)S(1)}, f32[1,4096,120]{1,2,0:T(8,128)}, u32[]{:S(2)}) copy-start(f32[1,4096,120]{1,2,0:T(8,128)} %param.11) | copy-start | bytes 5898244
  2.2 1.2 copy-start.1
  3.4 0.9 copy-start.2
  4.3 0.9 copy-start.3
  5.3 0.9 copy-start.4
  6.2 0.7 copy-start.5

commit v2 on v1

--- a/solution.py
+++ b/solution.py
@@ -20,12 +20,33 @@
 SUBS = PART // THIRD
 
 SLOT = {0: 0, 4: 1, 1: 2, -1: 3, 2: 4, -2: 5, 3: 6, -3: 7}
+SPREAD = (0, 2, -2)
+STEPS = (
+    [(0, 1), (1, 0), (-1, 0), (0, 2), (2, 0), (-2, 0), (0, 3)]
+    + [(1, 1), (-1, 1), (0,), (1, 2), (-1, 2), (2, 1), (-2, 1), (3, 0), (-3, 0), (1, 3), (-1, 3)]
+    + [(2, 2), (-2, 2), ((1, -1),), (3, 1), (-3, 1), (2, 3), (-2, 3), (3, 2), (-3, 2), ((2, -2),)]
+    + [(4, 0), (4, 1), (3, 3), (-3, 3), ((3, -3),), (4, 2), (4, 3)]
+)
+BLOCKS = [(0, 0)] + [step for step in STEPS if len(step) == 2]
+
+
+def y_hops(rel, k):
+    hops = []
+    for way, after in ((0, rel - 1), (1, rel + 1)):
+        if rel == 4 or (rel > 0) == (way == 0) and rel != 0:
+            continue
+        if abs(after) == 4:
+            if (k < 2) == (way == 0):
+                hops.append((way, 4))
+        elif k == 0 or after not in SPREAD:
+            hops.append((way, after))
+    return hops
 
 
 def body(
     tok_in, up_in, og_in, w_in, mom_in, table, live, out,
     tok, up, og, w, mom, acc, psend, precv, asend, arecv, fresh, share, inv,
-    load_sem, own_sem, z_send, z_recv, y_send, y_recv, c_send, c_recv,
+    load_sem, own_sem, t_send, t_recv, c_send, c_recv,
     p_send, p_recv, a_send, a_recv, out_sem,
 ):
     path = lax.axis_index("path")
@@ -41,6 +62,7 @@
 
     order = (z, z + 1 - 2 * (z % 2), 2 - z // 2, 3 - 3 * (z // 2))
     up_y, down_y = at((y + 1) % NY, z, core), at((y + NY - 1) % NY, z, core)
+    up_z, down_z = at(y, (z + 1) % ZL, core), at(y, (z + ZL - 1) % ZL, core)
     sibling = at(y, z, 1 - core)
 
     loads = [
@@ -51,52 +73,42 @@
     def rows(rel, k):
         return pl.ds(pl.multiple_of(SLOT[rel] * BUNDLE + (order[k] * 2 + core) * ROWS, ROWS), ROWS)
 
-    own = pltpu.make_async_copy(tok_in, tok.at[rows(0, 0)], own_sem)
+    own = pltpu.make_async_copy(tok_in, tok.at[rows(0, 0)], t_recv.at[SLOT[0], z])
     own.start()
     for load in loads:
         load.start()
 
     barrier = pltpu.get_barrier_semaphore()
-    friends = [up_y, down_y, sibling]
-    friends += [at(y, order[k], core) for k in range(1, ZL)]
+    friends = [up_y, down_y, up_z, down_z, sibling]
     friends += [((path + o) % NP, fsdp) for o in range(1, NP)]
     for friend in friends:
         pl.semaphore_signal(barrier, inc=1, device_id=friend, device_id_type=MESH)
     pl.semaphore_wait(barrier, len(friends))
 
-    def z_copy(k):
-        return pltpu.make_async_remote_copy(
-            src_ref=tok_in, dst_ref=tok.at[rows(0, 0)], send_sem=z_send.at[k], recv_sem=z_recv.at[z],
-            device_id=at(y, order[k], core), device_id_type=MESH,
-        )
-
-    def z_arrival(k):
-        return pltpu.make_async_remote_copy(
-            src_ref=tok_in, dst_ref=tok.at[rows(0, k)], send_sem=z_send.at[k], recv_sem=z_recv.at[order[k]],
-            device_id=at(y, order[k], core), device_id_type=MESH,
-        )
-
-    def y_copy(way, step, k):
-        sign = (-1, 1)[way]
-        before, after = sign * (step - 1), sign * step
-        after = 4 if after == -4 else after
-        src = tok_in if step == 1 and k == 0 else tok.at[rows(before, k)]
-        return pltpu.make_async_remote_copy(
-            src_ref=src, dst_ref=tok.at[rows(after, k)],
-            send_sem=y_send.at[way, step - 1, k], recv_sem=y_recv.at[way, step - 1, k],
-            device_id=(up_y, down_y)[way], device_id_type=MESH,
+    def source(rel, k):
+        return tok_in if rel == 0 and k == 0 else tok.at[rows(rel, k)]
+
+    def t_copy(link, rel, k, after):
+        return pltpu.make_async_remote_copy(
+            src_ref=source(rel, k), dst_ref=tok.at[rows(after, k)],
+            send_sem=t_send.at[link, SLOT[rel], order[k]], recv_sem=t_recv.at[SLOT[after], order[k]],
+            device_id=(up_y, down_y, up_z, down_z)[link], device_id_type=MESH,
         )
 
     def c_copy(rel, k):
-        src = tok_in if rel == 0 and k == 0 else tok.at[rows(rel, k)]
-        return pltpu.make_async_remote_copy(
-            src_ref=src, dst_ref=tok.at[rows(rel, k)],
-            send_sem=c_send.at[SLOT[rel], k], recv_sem=c_recv.at[SLOT[rel], k],
+        return pltpu.make_async_remote_copy(
+            src_ref=source(rel, k), dst_ref=tok.at[rows(rel, k)],
+            send_sem=c_send.at[SLOT[rel], order[k]], recv_sem=c_recv.at[SLOT[rel], order[k]],
             device_id=sibling, device_id_type=MESH,
         )
 
-    def sent(way, step, k):
-        return step < 4 or (k < 2) == (way == 0)
+    def for_hops(rel, k, act):
+        for way, after in y_hops(rel, k):
+            act(t_copy(way, rel, k, after))
+        if rel in SPREAD:
+            pl.when((order[k] <= z) & (z < ZL - 1))(lambda: act(t_copy(2, rel, k, rel)))
+            pl.when((order[k] >= z) & (z > 0))(lambda: act(t_copy(3, rel, k, rel)))
+        act(c_copy(rel, k))
 
     def gate_and_grad(rels, first):
         start, count = SLOT[rels[0]] * BUNDLE, len(rels) * BUNDLE
@@ -129,11 +141,7 @@
         for k in range(ZL):
             c_copy(rel, k).wait_recv()
 
-    for k in range(1, ZL):
-        z_copy(k).start()
-    for way in (0, 1):
-        y_copy(way, 1, 0).start()
-    c_copy(0, 0).start()
+    for_hops(0, 0, lambda copy: copy.start())
     for g in range(NP):
         total = jnp.float32(0.0)
         for h in range(NP):
@@ -142,35 +150,17 @@
             total = total + same
         inv[g] = 1.0 / total
     own.wait()
-    for k in range(1, ZL):
-        z_arrival(k).wait_recv()
-        for way in (0, 1):
-            y_copy(way, 1, k).start()
-        c_copy(0, k).start()
     for load in loads[:3]:
         load.wait()
-
-    def ring(step):
-        for k in range(ZL):
-            for way in (0, 1):
-                if sent(way, step, k):
-                    y_copy(way, step, k).wait_recv()
-                    if step < 4 and sent(way, step + 1, k):
-                        y_copy(way, step + 1, k).start()
-                    c_copy((-1, 1)[way] * step if step < 4 else 4, k).start()
-
-    wait_sibling(0)
-    accumulate((0,), True)
-    for step in (1, 2, 3):
-        ring(step)
-        if step > 1:
-            wait_sibling(step - 1)
-            wait_sibling(1 - step)
-            accumulate((step - 1, 1 - step), False)
-    wait_sibling(3)
-    wait_sibling(-3)
-    accumulate((3, -3), False)
-    ring(4)
+    for step in STEPS:
+        if len(step) == 2:
+            t_copy(0, step[0], step[1], step[0]).wait_recv()
+            for_hops(*step, lambda copy: copy.start())
+        else:
+            rels = step[0] if isinstance(step[0], tuple) else step
+            for rel in rels:
+                wait_sibling(rel)
+            accumulate(rels, rels == (0,))
     wait_sibling(4)
 
     def p_copy(chunk, dest):
@@ -246,7 +236,6 @@
             a_copy(chunk, (path + o) % NP).start()
 
     loads[3].wait()
-    writes = []
     for chunk in range(CHUNKS):
         mine = pltpu.make_async_copy(asend.at[chunk, path], arecv.at[chunk, path], own_sem)
         mine.start()
@@ -269,16 +258,8 @@
     write = pltpu.make_async_copy(fresh, out, out_sem)
     write.start()
 
-    for k in range(1, ZL):
-        z_copy(k).wait_send()
-    for step in range(1, 5):
-        for k in range(ZL):
-            for way in (0, 1):
-                if sent(way, step, k):
-                    y_copy(way, step, k).wait_send()
-    for rel in SLOT:
-        for k in range(ZL):
-            c_copy(rel, k).wait_send()
+    for block in BLOCKS:
+        for_hops(*block, lambda copy: copy.wait_send())
     for chunk in range(CHUNKS):
         for o in range(1, NP):
             p_copy(chunk, (path + o) % NP).wait_send()
@@ -310,15 +291,14 @@
             pltpu.SMEM((NP,), f32),
             dma((4,)),
             dma,
-            dma((ZL,)), dma((ZL,)),
-            dma((2, 4, ZL)), dma((2, 4, ZL)),
+            dma((4, NY, ZL)), dma((NY, ZL)),
             dma((NY, ZL)), dma((NY, ZL)),
             dma((CHUNKS, NP)), dma((CHUNKS, NP)),
             dma((CHUNKS, NP)), dma((CHUNKS, NP)),
             dma,
         ],
         compiler_params=pltpu.CompilerParams(
-            collective_id=0, has_side_effects=True, vmem_limit_bytes=40 * 2**20
+            collective_id=0, has_side_effects=True, vmem_limit_bytes=62 * 2**20
         ),
         name="outer_step",
     )(

time: 141 us -> 130 us (0.922)
  Pallas kernels: 132 us -> 124 us
  local copies, waits for them, and re-layouts: 7.13 us -> 2.23 us
    pallas_call x1, Pallas kernels: 132 us -> 124 us  [on_device(): pl.pallas_call(body, out_shape=jax.ShapeDtypeStruct((COLS, D), bf16), in_...]
    unnamed x13 -> x1, local copies, waits for them, and re-layouts: 7.13 us -> 2.23 us
where the time goes in v2:
time: 130 us; the launch traced here: 127 us
  Pallas kernels  124 us (95%)
  local copies, waits for them, and re-layouts  2.23 us (2%)
    pallas_call x1, Pallas kernels, on_device(): pl.pallas_call(body, out_shape=jax.ShapeDtypeStruct((COLS, D), bf16), in_...  124 us

profile of v2, /device:TPU:56, one launch (start us, length us, event | category | flops | bytes accessed | tf_op | source)
XLA Modules:
  0.0 127.4 jit_solution(15602947037519722795)
XLA Ops:
  0.7 124.5 %outer_step.1 = bf16[120,4096]{1,0:T(8,128)(2,1)} custom-call(bf16[16,4096]{1,0:T(8,128)(2,1)} %bitcast.22, bf16[120,1024]{1,0:T(8,128)(2,1)} %bitcast.20, bf16[120,1024]{1,0:T(8,128)(2,1)} %bitcast.21, bf16[120,4096]{1,0:T(8,128)(2,1)} %bitcast.19, f32[120,4096]{1,0:T(8,128)} %bitcast.18, s32[12]{0:T(128)} %bitcast.23, s32[1]{0:T(128)S(6)} %copy.9.live), custom_call_target="tpu_custom_call" | custom-call | tf_op jit(solution)/shard_map/outer_step/pallas_call | solution.py:276
  125.1 2.2 %copy.10 = bf16[1,4096,120]{1,2,0:T(8,128)(2,1)} copy(bf16[1,4096,120]{1,2,0:T(8,128)(2,1)} %bitcast.17) | data formatting | bytes 1966080

commit v3 on v2

--- a/solution.py
+++ b/solution.py
@@ -1,3 +1,5 @@
+import functools
+
 import jax
 import jax.numpy as jnp
 from jax import lax
@@ -14,11 +16,6 @@
 BUNDLE = ROWS * ZL * 2
 QUARTER = D // NX
 THIRD = COLS // ZH
-CHUNKS = 2
-LANES = 256
-PART = THIRD * QUARTER // (CHUNKS * LANES)
-SUBS = PART // THIRD
-
 SLOT = {0: 0, 4: 1, 1: 2, -1: 3, 2: 4, -2: 5, 3: 6, -3: 7}
 SPREAD = (0, 2, -2)
 STEPS = (
@@ -44,11 +41,14 @@
 
 
 def body(
-    tok_in, up_in, og_in, w_in, mom_in, table, live, out,
-    tok, up, og, w, mom, acc, psend, precv, asend, arecv, fresh, share, inv,
+    slots, chunks, lanes_of, tok_in, up_in, og_in, w_in, mom_in, table, live, out,
+    tok, up, og, w, mom, acc, psend, precv, asend, arecv, zbuf, fresh, share, inv, module,
     load_sem, own_sem, t_send, t_recv, c_send, c_recv,
-    p_send, p_recv, a_send, a_recv, out_sem,
+    p_send, p_recv, a_send, a_recv, z_send, z_recv, out_sem,
 ):
+    part_rows = THIRD * QUARTER // (chunks * lanes_of)
+    subs = part_rows // THIRD
+    width = subs * lanes_of
     path = lax.axis_index("path")
     fsdp = lax.axis_index("fsdp")
     core = fsdp % 2
@@ -80,7 +80,11 @@
 
     barrier = pltpu.get_barrier_semaphore()
     friends = [up_y, down_y, up_z, down_z, sibling]
-    friends += [((path + o) % NP, fsdp) for o in range(1, NP)]
+    if slots is None:
+        friends += [((path + o) % NP, fsdp) for o in range(1, NP)]
+    else:
+        friends += [((x + o) % NX * ZH + third, fsdp) for o in range(1, NX)]
+        friends += [(x * ZH + (third + o) % ZH, fsdp) for o in range(1, ZH)]
     for friend in friends:
         pl.semaphore_signal(barrier, inc=1, device_id=friend, device_id_type=MESH)
     pl.semaphore_wait(barrier, len(friends))
@@ -142,13 +146,63 @@
             c_copy(rel, k).wait_recv()
 
     for_hops(0, 0, lambda copy: copy.start())
-    for g in range(NP):
-        total = jnp.float32(0.0)
-        for h in range(NP):
-            same = jnp.where(table[g] == table[h], 1.0, 0.0).astype(jnp.float32)
-            share[g * NP + h] = same
-            total = total + same
-        inv[g] = 1.0 / total
+    def one_if(condition):
+        return jnp.where(condition, 1.0, 0.0).astype(jnp.float32)
+
+    def members(name):
+        return functools.reduce(lambda a, b: a + b, [one_if(table[h] == name) for h in range(NP)])
+
+    if slots is None:
+        for g in range(NP):
+            for h in range(NP):
+                share[g * NP + h] = one_if(table[g] == table[h])
+            inv[g] = 1.0 / members(table[g])
+    else:
+        for r in range(ZH):
+            names = [-1 - r * slots - j for j in range(slots)]
+            taken = jnp.int32(0)
+            for xx in range(NX):
+                name = table[xx * ZH + r]
+                abroad = functools.reduce(
+                    jnp.logical_or, [table[g] == name for g in range(NP) if g % ZH != r]
+                )
+                fresh_name = abroad
+                for before in range(xx):
+                    fresh_name = fresh_name & (table[before * ZH + r] != name)
+                names = [jnp.where(fresh_name & (taken == j), name, old) for j, old in enumerate(names)]
+                taken = taken + jnp.where(fresh_name, 1, 0)
+            for j in range(slots):
+                module[r * slots + j] = names[j]
+        mine = [table[xx * ZH + third] for xx in range(NX)]
+        planes = [(third + o) % ZH for o in range(1, ZH)]
+        here = [module[third * slots + j] for j in range(slots)]
+        there = [[module[r * slots + j] for j in range(slots)] for r in planes]
+        count = 0
+
+        def keep(values):
+            nonlocal count
+            at_ = count
+            for value in values:
+                share[count] = value
+                count += 1
+            return [share[at_ + i] for i in range(len(values))]
+
+        partial_of = [keep([one_if(name == here[j]) for name in mine]) for j in range(slots)]
+
+        def total_of(wanted):
+            scale = 1.0 / jnp.maximum(members(wanted), 1.0)
+            terms = [one_if(name == wanted) for name in mine]
+            terms += [one_if(name == wanted) for names in there for name in names]
+            return keep([term * scale for term in terms])
+
+        totals_of = [[total_of(there[i][j]) for j in range(slots)] for i in range(ZH - 1)]
+        averages_of = [total_of(mine[g]) for g in range(NX)]
+        spread_of = []
+        for g in range(NX):
+            picks = [one_if(mine[g] == here[j]) for j in range(slots)]
+            alone = 1.0 - functools.reduce(lambda a, b: a + b, picks)
+            scale = alone / members(mine[g])
+            spread_of.append(keep(picks + [one_if(name == mine[g]) * scale for name in mine]))
     own.wait()
     for load in loads[:3]:
         load.wait()
@@ -163,88 +217,186 @@
             accumulate(rels, rels == (0,))
     wait_sibling(4)
 
+    def remote(src, dst, send_sem, recv_sem, to):
+        return pltpu.make_async_remote_copy(
+            src_ref=src, dst_ref=dst, send_sem=send_sem, recv_sem=recv_sem, device_id=(to, fsdp), device_id_type=MESH
+        )
+
     def p_copy(chunk, dest):
-        return pltpu.make_async_remote_copy(
-            src_ref=psend.at[chunk, dest], dst_ref=precv.at[chunk, path],
-            send_sem=p_send.at[chunk, dest], recv_sem=p_recv.at[chunk, path],
-            device_id=(dest, fsdp), device_id_type=MESH,
+        return remote(
+            psend.at[chunk, dest], precv.at[chunk, path], p_send.at[chunk, dest], p_recv.at[chunk, path], dest
         )
 
     def p_arrival(chunk, source):
-        return pltpu.make_async_remote_copy(
-            src_ref=psend.at[chunk, source], dst_ref=precv.at[chunk, source],
-            send_sem=p_send.at[chunk, source], recv_sem=p_recv.at[chunk, source],
-            device_id=(source, fsdp), device_id_type=MESH,
+        return remote(
+            psend.at[chunk, source], precv.at[chunk, source], p_send.at[chunk, source], p_recv.at[chunk, source], source
         )
 
     def a_copy(chunk, dest):
-        return pltpu.make_async_remote_copy(
-            src_ref=asend.at[chunk, dest], dst_ref=arecv.at[chunk, path],
-            send_sem=a_send.at[chunk, dest], recv_sem=a_recv.at[chunk, path],
-            device_id=(dest, fsdp), device_id_type=MESH,
+        return remote(
+            asend.at[chunk, dest], arecv.at[chunk, path], a_send.at[chunk, dest], a_recv.at[chunk, path], dest
         )
 
     def a_arrival(chunk, source):
-        return pltpu.make_async_remote_copy(
-            src_ref=asend.at[chunk, source], dst_ref=arecv.at[chunk, source],
-            send_sem=a_send.at[chunk, source], recv_sem=a_recv.at[chunk, source],
-            device_id=(source, fsdp), device_id_type=MESH,
+        return remote(
+            asend.at[chunk, source], arecv.at[chunk, source], a_send.at[chunk, source], a_recv.at[chunk, source], source
+        )
+
+    def of_x(xx):
+        return pl.ds(xx * ZH, ZH)
+
+    def x_copy(back, chunk, dest, landing):
+        out_buf, in_buf, out_sem_, in_sem = ((psend, precv, p_send, p_recv), (asend, arecv, a_send, a_recv))[back]
+        return remote(
+            out_buf.at[chunk, of_x(dest)], in_buf.at[chunk, of_x(landing)],
+            out_sem_.at[chunk, dest], in_sem.at[chunk, landing], dest * ZH + third,
+        )
+
+    def z_copy(back, chunk, o):
+        return remote(
+            zbuf.at[2 * back, chunk, o - 1], zbuf.at[2 * back + 1, chunk, ZH - 1 - o],
+            z_send.at[back, chunk, o - 1], z_recv.at[back, chunk, ZH - 1 - o],
+            x * ZH + (third + o) % ZH,
         )
 
     start, count, grad = gate_and_grad((4,), False)
-    for j in range(NX):
-        q = (x + j) % NX
-        lanes = pl.ds(pl.multiple_of(q * QUARTER, QUARTER), QUARTER)
-        total = acc[:, lanes] + jnp.dot(grad, tok[start : start + count, lanes], preferred_element_type=jnp.float32)
-        total = total * (1.0 / D**0.5)
-        for chunk in range(CHUNKS):
-            for i in range(ZH):
-                r = (third + 1 + i) % ZH
-                dest = q * ZH + r
-                first = chunk * SUBS * LANES
-                for rr in range(ZH):
-                    piece = jnp.concatenate(
-                        [
-                            total[rr * THIRD : (rr + 1) * THIRD, first + s * LANES : first + (s + 1) * LANES]
-                            for s in range(SUBS)
-                        ],
-                        axis=0,
-                    ).astype(jnp.bfloat16)
-                    if i == 0:
-                        psend[chunk, q * ZH + rr] = piece
-                if j > 0 or i < ZH - 1:
-                    p_copy(chunk, dest).start()
-
-    for chunk in range(CHUNKS):
+
+    def last_products(chunk):
+        for j in (1, 2, 3, 0):
+            q = (x + j) % NX
+            first = pl.multiple_of(q * QUARTER + chunk * width, width)
+            lanes = pl.ds(first, width)
+            total = acc[:, lanes] + jnp.dot(
+                grad, tok[start : start + count, lanes], preferred_element_type=jnp.float32
+            )
+            total = total * (1.0 / D**0.5)
+            for r in range(ZH):
+                piece = jnp.concatenate(
+                    [
+                        total[r * THIRD : (r + 1) * THIRD, s * lanes_of : (s + 1) * lanes_of]
+                        for s in range(subs)
+                    ],
+                    axis=0,
+                ).astype(jnp.bfloat16)
+                if slots is not None and j == 0:
+                    precv[chunk, q * ZH + r] = piece
+                else:
+                    psend[chunk, q * ZH + r] = piece
+            if slots is None:
+                for i in range(ZH - 1 if j == 0 else ZH):
+                    p_copy(chunk, q * ZH + (third + 1 + i) % ZH).start()
+            elif j > 0 and chunk == 0:
+                x_copy(0, chunk, q, x).start()
+
+    for chunk in range(chunks):
+        last_products(chunk)
+    if slots is not None:
+        for o in range(1, NX):
+            x_copy(0, 1, (x + o) % NX, x).start()
+
+    def combine(coefficients, values):
+        total = coefficients[0] * values[0]
+        for c, v in zip(coefficients[1:], values[1:]):
+            total = total + c * v
+        return total
+
+    def row_tiles(work):
+        @pl.loop(0, part_rows // 16)
+        def _(i):
+            work(pl.ds(pl.multiple_of(i * 16, 16), 16))
+
+    def f32(value):
+        return value.astype(jnp.float32)
+
+    def own_copy(chunk):
+        if slots is None:
+            return pltpu.make_async_copy(asend.at[chunk, path], arecv.at[chunk, path], own_sem.at[chunk])
+        return pltpu.make_async_copy(asend.at[chunk, of_x(x)], arecv.at[chunk, of_x(x)], own_sem.at[chunk])
+
+    def own_average(chunk):
         for o in range(1, NP):
             p_arrival(chunk, (path + o) % NP).wait_recv()
-        mine = pltpu.make_async_copy(psend.at[chunk, path], precv.at[chunk, path], own_sem)
-        mine.start()
-        mine.wait()
-
-        @pl.loop(0, PART // 16)
-        def _(i):
-            part = pl.ds(pl.multiple_of(i * 16, 16), 16)
-            values = [precv[chunk, h, part].astype(jnp.float32) for h in range(NP)]
+        mine_ = pltpu.make_async_copy(psend.at[chunk, path], precv.at[chunk, path], own_sem.at[chunk])
+        mine_.start()
+        mine_.wait()
+
+        def work(part):
+            values = [f32(precv[chunk, h, part]) for h in range(NP)]
             for g in range(NP):
-                total = share[g * NP] * values[0]
-                for h in range(1, NP):
-                    total = total + share[g * NP + h] * values[h]
+                total = combine([share[g * NP + h] for h in range(NP)], values)
                 asend[chunk, g, part] = (total * inv[g]).astype(jnp.bfloat16)
 
+        row_tiles(work)
+        own_copy(chunk).start()
         for o in range(1, NP):
             a_copy(chunk, (path + o) % NP).start()
 
-    loads[3].wait()
-    for chunk in range(CHUNKS):
-        mine = pltpu.make_async_copy(asend.at[chunk, path], arecv.at[chunk, path], own_sem)
-        mine.start()
-        mine.wait()
-        for o in range(1, NP):
-            a_arrival(chunk, (path + o) % NP).wait_recv()
+    def partial_sums(chunk):
+        for o in range(1, NX):
+            x_copy(0, chunk, (x + o) % NX, (x + o) % NX).wait_recv()
+        if chunk + 2 < chunks:
+            for o in range(1, NX):
+                x_copy(0, chunk + 2, (x + o) % NX, x).start()
+
+        def work(part):
+            for i, r in enumerate(planes):
+                values = [f32(precv[chunk, g * ZH + r, part]) for g in range(NX)]
+                for j in range(slots):
+                    zbuf[0, chunk, i, j, part] = combine(partial_of[j], values).astype(jnp.bfloat16)
+
+        row_tiles(work)
+        for o in range(1, ZH):
+            z_copy(0, chunk, o).start()
+
+    def totals(chunk):
+        for o in range(1, ZH):
+            z_copy(0, chunk, o).wait_recv()
+
+        def work(part):
+            values = [f32(precv[chunk, g * ZH + third, part]) for g in range(NX)]
+            values += [f32(zbuf[1, chunk, i, j, part]) for i in range(ZH - 1) for j in range(slots)]
+            for i in range(ZH - 1):
+                for j in range(slots):
+                    zbuf[2, chunk, i, j, part] = combine(totals_of[i][j], values).astype(jnp.bfloat16)
+            for g in range(NX):
+                asend[chunk, g * ZH + third, part] = combine(averages_of[g], values).astype(jnp.bfloat16)
+
+        row_tiles(work)
+        for o in range(1, ZH):
+            z_copy(1, chunk, o).start()
+
+    def spread(chunk):
+        for o in range(1, ZH):
+            z_copy(1, chunk, o).wait_recv()
+
+        def work(part):
+            for i, r in enumerate(planes):
+                values = [f32(zbuf[3, chunk, i, j, part]) for j in range(slots)]
+                values += [f32(precv[chunk, g * ZH + r, part]) for g in range(NX)]
+                for g in range(NX):
+                    asend[chunk, g * ZH + r, part] = combine(spread_of[g], values).astype(jnp.bfloat16)
+
+        row_tiles(work)
+        for o in range(1, NX):
+            x_copy(1, chunk, (x + o) % NX, x).start()
+        own_copy(chunk).start()
+
+    def write(chunk, q):
+        lanes = slice(q * QUARTER + chunk * width, q * QUARTER + (chunk + 1) * width)
+        return pltpu.make_async_copy(fresh.at[:, lanes], out.at[:, lanes], out_sem.at[chunk, q])
+
+    def update(chunk):
+        own_copy(chunk).wait()
+        if slots is None:
+            for o in range(1, NP):
+                a_arrival(chunk, (path + o) % NP).wait_recv()
+        else:
+            for o in range(1, NX):
+                x_copy(1, chunk, (x + o) % NX, (x + o) % NX).wait_recv()
         for q in range(NX):
-            for s in range(SUBS):
-                lanes = slice(q * QUARTER + (chunk * SUBS + s) * LANES, q * QUARTER + (chunk * SUBS + s + 1) * LANES)
+            for s in range(subs):
+                first = q * QUARTER + chunk * width + s * lanes_of
+                lanes = slice(first, first + lanes_of)
                 averaged = jnp.concatenate(
                     [
                         arecv[chunk, q * ZH + r].astype(jnp.float32)[s * THIRD : (s + 1) * THIRD]
@@ -255,26 +407,50 @@
                 moment = 0.9 * mom[:, lanes] + averaged
                 new = w[:, lanes].astype(jnp.float32) - 0.7 * (averaged + 0.9 * moment)
                 fresh[:, lanes] = new.astype(jnp.bfloat16)
-    write = pltpu.make_async_copy(fresh, out, out_sem)
-    write.start()
+            write(chunk, q).start()
+
+    loads[3].wait()
+    if slots is None:
+        for chunk in range(chunks):
+            own_average(chunk)
+        for chunk in range(chunks):
+            update(chunk)
+    else:
+        for chunk in range(chunks):
+            partial_sums(chunk)
+        for step in range(chunks + 2):
+            for late, act in ((0, totals), (1, spread), (2, update)):
+                if 0 <= step - late < chunks:
+                    act(step - late)
 
     for block in BLOCKS:
         for_hops(*block, lambda copy: copy.wait_send())
-    for chunk in range(CHUNKS):
-        for o in range(1, NP):
-            p_copy(chunk, (path + o) % NP).wait_send()
-            a_copy(chunk, (path + o) % NP).wait_send()
-    write.wait()
-
-
-def on_device(tokens, up_values, out_grad, weights, momentum, path_table, live_tokens):
+    for chunk in range(chunks):
+        if slots is None:
+            for o in range(1, NP):
+                p_copy(chunk, (path + o) % NP).wait_send()
+                a_copy(chunk, (path + o) % NP).wait_send()
+        else:
+            for back in (0, 1):
+                for o in range(1, NX):
+                    x_copy(back, chunk, (x + o) % NX, x).wait_send()
+                for o in range(1, ZH):
+                    z_copy(back, chunk, o).wait_send()
+    for chunk in range(chunks):
+        for q in range(NX):
+            write(chunk, q).wait()
+
+
+def outer_step(slots, number, *arrays):
     dma = pltpu.SemaphoreType.DMA
     bf16, f32 = jnp.bfloat16, jnp.float32
     anywhere = pl.BlockSpec(memory_space=pl.ANY)
     scalars = pl.BlockSpec(memory_space=pltpu.SMEM)
-    shard = pltpu.VMEM((CHUNKS, NP, PART, LANES), bf16)
-    new = pl.pallas_call(
-        body,
+    chunks, lanes_of = (2, 256) if slots is None else (4, 128)
+    part_rows = THIRD * QUARTER // (chunks * lanes_of)
+    shard = pltpu.VMEM((chunks, NP, part_rows, lanes_of), bf16)
+    return pl.pallas_call(
+        functools.partial(body, slots, chunks, lanes_of),
         out_shape=jax.ShapeDtypeStruct((COLS, D), bf16),
         in_specs=[anywhere] * 5 + [scalars] * 2,
         out_specs=anywhere,
@@ -286,24 +462,53 @@
             pltpu.VMEM((COLS, D), f32),
             pltpu.VMEM((COLS, D), f32),
             shard, shard, shard, shard,
+            pltpu.VMEM((4, chunks, ZH - 1, slots or 1, part_rows, lanes_of), bf16),
             pltpu.VMEM((COLS, D), bf16),
             pltpu.SMEM((NP * NP,), f32),
             pltpu.SMEM((NP,), f32),
+            pltpu.SMEM((NP,), jnp.int32),
             dma((4,)),
-            dma,
+            dma((chunks,)),
             dma((4, NY, ZL)), dma((NY, ZL)),
             dma((NY, ZL)), dma((NY, ZL)),
-            dma((CHUNKS, NP)), dma((CHUNKS, NP)),
-            dma((CHUNKS, NP)), dma((CHUNKS, NP)),
-            dma,
+            dma((chunks, NP)), dma((chunks, NP)),
+            dma((chunks, NP)), dma((chunks, NP)),
+            dma((2, chunks, ZH - 1)), dma((2, chunks, ZH - 1)),
+            dma((chunks, NX)),
         ],
         compiler_params=pltpu.CompilerParams(
-            collective_id=0, has_side_effects=True, vmem_limit_bytes=62 * 2**20
+            collective_id=number, has_side_effects=True, vmem_limit_bytes=62 * 2**20
         ),
         name="outer_step",
-    )(
-        tokens[0], up_values[0].T, out_grad[0].T, weights[0].T, momentum[0].T,
-        path_table[:, 0], live_tokens,
+    )(*arrays)
+
+
+def widest_plane(table, most):
+    result = jnp.int32(0)
+    for r in range(ZH):
+        shared = jnp.int32(0)
+        for xx in range(NX):
+            name = table[xx * ZH + r]
+            counts = functools.reduce(jnp.logical_or, [table[g] == name for g in range(NP) if g % ZH != r])
+            for before in range(xx):
+                counts = counts & (table[before * ZH + r] != name)
+            shared = shared + jnp.where(counts, 1, 0)
+        result = jnp.maximum(result, shared)
+    most[0] = jnp.maximum(result, 2) - 2
+
+
+def on_device(tokens, up_values, out_grad, weights, momentum, path_table, live_tokens):
+    scalars = pl.BlockSpec(memory_space=pltpu.SMEM)
+    table = path_table[:, 0]
+    most = pl.pallas_call(
+        widest_plane, out_shape=jax.ShapeDtypeStruct((1,), jnp.int32),
+        in_specs=[scalars], out_specs=scalars, name="widest_plane",
+    )(table)[0]
+    arrays = (tokens[0], up_values[0].T, out_grad[0].T, weights[0].T, momentum[0].T, table, live_tokens)
+    new = lax.switch(
+        most,
+        [functools.partial(outer_step, slots, number) for number, slots in enumerate((2, 3, None))],
+        *arrays,
     )
     return new.T[None]
 

time: 130 us -> 129 us (level); the launches traced: 127 us -> 129 us
  Pallas kernels: 124 us -> 127 us
    pallas_call x1 -> x2, Pallas kernels: 124 us -> 127 us  [the longest x1 125 us: outer_step(): pl.pallas_call(functools.partial(body, slots, chunks, lanes_of), out_shap...]
where the time goes in v3:
time: 129 us
  Pallas kernels  127 us (98%)
    pallas_call x1, Pallas kernels, outer_step(): pl.pallas_call(functools.partial(body, slots, chunks, lanes_of), out_shap...  125 us

profile of v3, /device:TPU:56, one launch (start us, length us, event | category | flops | bytes accessed | tf_op | source)
XLA Modules:
  0.0 129.0 jit_solution(1577994228392296741)
XLA Ops:
  0.0 1.3 widest_plane.1
  1.9 126.1 %conditional.1 = (bf16[120,4096]{1,0:T(8,128)(2,1)S(1)}) conditional(s32[]{:T(128)} %bitcast.1, (bf16[16,4096]{1,0:T(8,128)(2,1)}, bf16[120,1024]{1,0:T(8,128)(2,1)}, bf16[120,1024]{1,0:T(8,128)(2,1)}, bf16[120,4096]{1,0:T(8,128)(2,1)}, f32[120,4096]{1,0:T(8,128)}, /*index=5*/s32[12]{0:T(128)}, s32[1]{0:T(128)}) %tuple.33, ...), branch_computations={%region_0.0_spmd, %region_1.0_spmd, %region_2.0_spmd} | conditional | bytes 8 | solution.py:508
  2.2 125.4 %outer_step.4 = bf16[120,4096]{1,0:T(8,128)(2,1)S(1)} custom-call(bf16[16,4096]{1,0:T(8,128)(2,1)} %get-tuple-element.58.tok_in, bf16[120,1024]{1,0:T(8,128)(2,1)} %get-tuple-element.59.up_in, bf16[120,1024]{1,0:T(8,128)(2,1)} %get-tuple-element.60.og_in, bf16[120,4096]{1,0:T(8,128)(2,1)} %get-tuple-element.61.w_in, f32[120,4096]{1,0:T(8,128)} %get-tuple-element.62.mom_in, ...), custom_call_target="tpu_custom_call" | custom-call | tf_op jit(solution)/shard_map/cond/branch_1_fun/outer_step/pallas_call | solution.py:452
  128.0 0.9 copy.12

commit v4 on v3

--- a/solution.py
+++ b/solution.py
@@ -242,15 +242,29 @@
             asend.at[chunk, source], arecv.at[chunk, source], a_send.at[chunk, source], a_recv.at[chunk, source], source
         )
 
+    def turned(r):
+        return (r - third + ZH) % ZH
+
     def of_x(xx):
         return pl.ds(xx * ZH, ZH)
 
-    def x_copy(back, chunk, dest, landing):
+    def x_copy(back, chunk, dest, landing, others):
+        def of(xx):
+            return pl.ds(xx * ZH + 1, ZH - 1) if others else pl.ds(xx * ZH, 1)
+
         out_buf, in_buf, out_sem_, in_sem = ((psend, precv, p_send, p_recv), (asend, arecv, a_send, a_recv))[back]
         return remote(
-            out_buf.at[chunk, of_x(dest)], in_buf.at[chunk, of_x(landing)],
-            out_sem_.at[chunk, dest], in_sem.at[chunk, landing], dest * ZH + third,
-        )
+            out_buf.at[chunk, of(dest)], in_buf.at[chunk, of(landing)],
+            out_sem_.at[chunk, others * NX + dest], in_sem.at[chunk, others * NX + landing], dest * ZH + third,
+        )
+
+    def x_start(back, chunk, others):
+        for o in range(1, NX):
+            x_copy(back, chunk, (x + o) % NX, x, others).start()
+
+    def x_wait(back, chunk, others):
+        for o in range(1, NX):
+            x_copy(back, chunk, (x + o) % NX, (x + o) % NX, others).wait_recv()
 
     def z_copy(back, chunk, o):
         return remote(
@@ -278,21 +292,25 @@
                     ],
                     axis=0,
                 ).astype(jnp.bfloat16)
-                if slots is not None and j == 0:
-                    precv[chunk, q * ZH + r] = piece
+                if slots is None:
+                    psend[chunk, q * ZH + r] = piece
+                elif j == 0:
+                    precv[chunk, q * ZH + turned(r)] = piece
                 else:
-                    psend[chunk, q * ZH + r] = piece
+                    psend[chunk, q * ZH + turned(r)] = piece
             if slots is None:
                 for i in range(ZH - 1 if j == 0 else ZH):
                     p_copy(chunk, q * ZH + (third + 1 + i) % ZH).start()
             elif j > 0 and chunk == 0:
-                x_copy(0, chunk, q, x).start()
+                x_copy(0, chunk, q, x, 1).start()
+        if slots is not None and chunk == 0:
+            x_start(0, chunk, 0)
 
     for chunk in range(chunks):
         last_products(chunk)
     if slots is not None:
-        for o in range(1, NX):
-            x_copy(0, 1, (x + o) % NX, x).start()
+        for others in (1, 0):
+            x_start(0, 1, others)
 
     def combine(coefficients, values):
         total = coefficients[0] * values[0]
@@ -332,15 +350,14 @@
             a_copy(chunk, (path + o) % NP).start()
 
     def partial_sums(chunk):
-        for o in range(1, NX):
-            x_copy(0, chunk, (x + o) % NX, (x + o) % NX).wait_recv()
+        x_wait(0, chunk, 1)
         if chunk + 2 < chunks:
-            for o in range(1, NX):
-                x_copy(0, chunk + 2, (x + o) % NX, x).start()
+            for others in (1, 0):
+                x_start(0, chunk + 2, others)
 
         def work(part):
-            for i, r in enumerate(planes):
-                values = [f32(precv[chunk, g * ZH + r, part]) for g in range(NX)]
+            for i in range(ZH - 1):
+                values = [f32(precv[chunk, g * ZH + 1 + i, part]) for g in range(NX)]
                 for j in range(slots):
                     zbuf[0, chunk, i, j, part] = combine(partial_of[j], values).astype(jnp.bfloat16)
 
@@ -351,34 +368,35 @@
     def totals(chunk):
         for o in range(1, ZH):
             z_copy(0, chunk, o).wait_recv()
+        x_wait(0, chunk, 0)
 
         def work(part):
-            values = [f32(precv[chunk, g * ZH + third, part]) for g in range(NX)]
+            values = [f32(precv[chunk, g * ZH, part]) for g in range(NX)]
             values += [f32(zbuf[1, chunk, i, j, part]) for i in range(ZH - 1) for j in range(slots)]
             for i in range(ZH - 1):
                 for j in range(slots):
                     zbuf[2, chunk, i, j, part] = combine(totals_of[i][j], values).astype(jnp.bfloat16)
             for g in range(NX):
-                asend[chunk, g * ZH + third, part] = combine(averages_of[g], values).astype(jnp.bfloat16)
+                asend[chunk, g * ZH, part] = combine(averages_of[g], values).astype(jnp.bfloat16)
 
         row_tiles(work)
         for o in range(1, ZH):
             z_copy(1, chunk, o).start()
+        x_start(1, chunk, 0)
 
     def spread(chunk):
         for o in range(1, ZH):
             z_copy(1, chunk, o).wait_recv()
 
         def work(part):
-            for i, r in enumerate(planes):
+            for i in range(ZH - 1):
                 values = [f32(zbuf[3, chunk, i, j, part]) for j in range(slots)]
-                values += [f32(precv[chunk, g * ZH + r, part]) for g in range(NX)]
+                values += [f32(precv[chunk, g * ZH + 1 + i, part]) for g in range(NX)]
                 for g in range(NX):
-                    asend[chunk, g * ZH + r, part] = combine(spread_of[g], values).astype(jnp.bfloat16)
+                    asend[chunk, g * ZH + 1 + i, part] = combine(spread_of[g], values).astype(jnp.bfloat16)
 
         row_tiles(work)
-        for o in range(1, NX):
-            x_copy(1, chunk, (x + o) % NX, x).start()
+        x_start(1, chunk, 1)
         own_copy(chunk).start()
 
     def write(chunk, q):
@@ -391,15 +409,15 @@
             for o in range(1, NP):
                 a_arrival(chunk, (path + o) % NP).wait_recv()
         else:
-            for o in range(1, NX):
-                x_copy(1, chunk, (x + o) % NX, (x + o) % NX).wait_recv()
+            x_wait(1, chunk, 0)
+            x_wait(1, chunk, 1)
         for q in range(NX):
             for s in range(subs):
                 first = q * QUARTER + chunk * width + s * lanes_of
                 lanes = slice(first, first + lanes_of)
                 averaged = jnp.concatenate(
                     [
-                        arecv[chunk, q * ZH + r].astype(jnp.float32)[s * THIRD : (s + 1) * THIRD]
+                        arecv[chunk, q * ZH + (r if slots is None else turned(r))].astype(jnp.float32)[s * THIRD : (s + 1) * THIRD]
                         for r in range(ZH)
                     ],
                     axis=0,
@@ -433,7 +451,8 @@
         else:
             for back in (0, 1):
                 for o in range(1, NX):
-                    x_copy(back, chunk, (x + o) % NX, x).wait_send()
+                    for others in (0, 1):
+                        x_copy(back, chunk, (x + o) % NX, x, others).wait_send()
                 for o in range(1, ZH):
                     z_copy(back, chunk, o).wait_send()
     for chunk in range(chunks):

time: 129 us -> 127 us (0.984)
  Pallas kernels: 127 us -> 124 us
    pallas_call x1, Pallas kernels: 125 us -> 123 us  [outer_step(): pl.pallas_call(functools.partial(body, slots, chunks, lanes_of), out_shap...]
where the time goes in v4:
time: 127 us; the launch traced here: 126 us
  Pallas kernels  124 us (98%)
    pallas_call x1, Pallas kernels, outer_step(): pl.pallas_call(functools.partial(body, slots, chunks, lanes_of), out_shap...  123 us

profile of v4, /device:TPU:56, one launch (start us, length us, event | category | flops | bytes accessed | tf_op | source)
XLA Modules:
  0.0 126.1 jit_solution(16345787622295204211)
XLA Ops:
  0.0 1.3 widest_plane.1
  1.9 123.2 %conditional.1 = (bf16[120,4096]{1,0:T(8,128)(2,1)S(1)}) conditional(s32[]{:T(128)} %bitcast.1, (bf16[16,4096]{1,0:T(8,128)(2,1)}, bf16[120,1024]{1,0:T(8,128)(2,1)}, bf16[120,1024]{1,0:T(8,128)(2,1)}, bf16[120,4096]{1,0:T(8,128)(2,1)}, f32[120,4096]{1,0:T(8,128)}, /*index=5*/s32[12]{0:T(128)}, s32[1]{0:T(128)}) %tuple.33, ...), branch_computations={%region_0.0_spmd, %region_1.0_spmd, %region_2.0_spmd} | conditional | bytes 8 | solution.py:527
  2.2 122.5 %outer_step.4 = bf16[120,4096]{1,0:T(8,128)(2,1)S(1)} custom-call(bf16[16,4096]{1,0:T(8,128)(2,1)} %get-tuple-element.58.tok_in, bf16[120,1024]{1,0:T(8,128)(2,1)} %get-tuple-element.59.up_in, bf16[120,1024]{1,0:T(8,128)(2,1)} %get-tuple-element.60.og_in, bf16[120,4096]{1,0:T(8,128)(2,1)} %get-tuple-element.61.w_in, f32[120,4096]{1,0:T(8,128)} %get-tuple-element.62.mom_in, ...), custom_call_target="tpu_custom_call" | custom-call | tf_op jit(solution)/shard_map/cond/branch_1_fun/outer_step/pallas_call | solution.py:471
  125.1 0.9 copy.12
